TPU v7x, 128 devices: a whole 4x4x4 slice. The times are simulated.
128 devices in a mesh: dp: 4 (over y), context: 8 (over z, x_hi), tensor: 4 (over x_lo, core).
Axes of the slice: x: 4 (x_hi: 2, x_lo: 2; x = x_hi * 2 + x_lo), y: 4, z: 4, core: 2. Of those that a mesh axis runs over, the one named last changes fastest.
Arguments:
- tokens: bfloat16 [8, 1024, 2048], P('dp', 'context'), may hold values from -6 to 6
- attn_gain: bfloat16 [2048], replicated, may hold values from 0.5 to 1.5
- w_query: bfloat16 [2048, 2048], P(None, 'tensor'), may hold values from -0.125 to 0.125
- w_key: bfloat16 [2048, 1024], P(None, 'tensor'), may hold values from -0.125 to 0.125
- w_value: bfloat16 [2048, 1024], P(None, 'tensor'), may hold values from -0.125 to 0.125
- query_gain: bfloat16 [128], replicated, may hold values from 0.25 to 1.75
- key_gain: bfloat16 [128], replicated, may hold values from 0.25 to 1.75
- w_out: bfloat16 [2048, 2048], P('tensor'), may hold values from -1.5 to 1.5
- mlp_gain: bfloat16 [2048], replicated, may hold values from 0.5 to 1.5
- w_gate: bfloat16 [2048, 6144], P(None, 'tensor'), may hold values from -0.125 to 0.125
- w_up: bfloat16 [2048, 6144], P(None, 'tensor'), may hold values from -0.125 to 0.125
- w_down: bfloat16 [6144, 2048], P('tensor'), may hold values from -0.078125 to 0.078125
- out_grad: bfloat16 [8, 1024, 2048], P('dp', 'context'), may hold values from -6 to 6
Outputs:
- block_out: bfloat16 [8, 1024, 2048], P('dp', 'context')
- tokens_grad: bfloat16 [8, 1024, 2048], P('dp', 'context')
- attn_gain_grad: float32 [2048], replicated
- w_query_grad: float32 [2048, 2048], P(('dp', 'context'), 'tensor')
- w_key_grad: float32 [2048, 1024], P(('dp', 'context'), 'tensor')
- w_value_grad: float32 [2048, 1024], P(('dp', 'context'), 'tensor')
- query_gain_grad: float32 [128], replicated
- key_gain_grad: float32 [128], replicated
- w_out_grad: float32 [2048, 2048], P('tensor', ('dp', 'context'))
- mlp_gain_grad: float32 [2048], replicated
- w_gate_grad: float32 [2048, 6144], P(('dp', 'context'), 'tensor')
- w_up_grad: float32 [2048, 6144], P(('dp', 'context'), 'tensor')
- w_down_grad: float32 [6144, 2048], P('tensor', ('dp', 'context'))
All inputs are finite; a program needn't handle non-finite values.
Results may differ from a plain program's by a relative error of at most 0.029.
Values may be sent and summed in bfloat16 or wider, within the bound.
A program may use at most 256 MiB of HBM per device.

v0:
```python
import numpy as np
import jax
import jax.numpy as jnp
from jax import lax
from jax.experimental import pallas as pl
from jax.experimental.pallas import tpu as pltpu
from jax.sharding import PartitionSpec as P

MESH = pl.DeviceIdType.MESH
BF = jnp.bfloat16
F32 = jnp.float32
EPSILON = 1e-06
ROPE_BASE = 1000000.0
SCALE = 128 ** (-0.5)


def me_place():
    c = lax.axis_index("context")
    return (lax.axis_index("dp"), c // 2, c % 2, lax.axis_index("tensor"))


def dev(place):
    y, z, h, t = place
    return (y, z * 2 + h, t)


def flip4(v, which):
    return v + 1 - 2 * (v % 2) if which == "0" else 3 - v


def pair_bit(y):
    return ((y + 1) // 2) % 2


def partner(place, dim):
    y, z, h, t = place
    if dim == "core":
        return (y, z, h, t + 1 - 2 * (t % 2))
    if dim == "xl":
        return (y, z, h, (t + 2) % 4)
    if dim == "xh":
        return (y, z, 1 - h, t)
    if dim[0] == "y":
        return (flip4(y, dim[1]), z, h, t)
    return (y, flip4(z, dim[1]), h, t)


def dot(a, b):
    return jnp.dot(a, b, preferred_element_type=F32)


def dot_nt(a, b):
    return lax.dot_general(a, b, (((1,), (1,)), ((), ())), preferred_element_type=F32)


def dot_tn(a, b):
    return lax.dot_general(a, b, (((0,), (0,)), ((), ())), preferred_element_type=F32)


def row_of(ref):
    return ref[...].astype(F32).reshape(1, -1)


def rows_at(start, n):
    return pl.ds(pl.multiple_of(start, min(n, 64)), n)


def own_rows(place, chunk, wide):
    y, _, _, t = place
    return rows_at(chunk * 256 + pair_bit(y) * 128 + t * 32 if wide else chunk * 128 + t * 32, 32)


def remote(src, dst, send_sem, recv_sem, place):
    return pltpu.make_async_remote_copy(src_ref=src, dst_ref=dst, send_sem=send_sem, recv_sem=recv_sem,
                                        device_id=dev(place), device_id_type=MESH)


def wait_bytes(view, sem):
    pltpu.make_async_copy(view, view, sem).wait()


def subsets(dims, place):
    found = [place]
    for dim in dims:
        found = found + [partner(p, dim) for p in found]
    return found


class GroupSum:
    def __init__(self, me, low, recvs, sems, wide):
        self.me, self.low, self.recvs, self.sems, self.wide = me, low, recvs, sems, wide

    def order(self, j):
        if not self.wide:
            return ("core", "xl")
        return (("core", "xl", "y0"), ("core", "y0", "xl"))[j]

    def copies(self, j, s):
        dims = self.order(j)
        to = partner(self.me, dims[s])
        return [remote(self.low.at[own_rows(block, j, self.wide)], self.recvs[s].at[j, i],
                       self.sems.at[s, j, i, 0], self.sems.at[s, j, i, 1], to)
                for i, block in enumerate(subsets(dims[s + 1:], to))]

    def send(self, j, s=0):
        for cp in self.copies(j, s):
            cp.start()

    def step(self, j, s):
        dims = self.order(j)
        for cp in self.copies(j, s):
            cp.wait_recv()
        for i, block in enumerate(subsets(dims[s + 1:], self.me)):
            r = own_rows(block, j, self.wide)
            v = self.low[r, :].astype(F32) + self.recvs[s][j, i].astype(F32)
            if s == len(dims) - 1:
                return v
            self.low[r, :] = v.astype(BF)
        self.send(j, s + 1)

    def finish(self):
        for j in range(2):
            for s in range(len(self.order(j))):
                for cp in self.copies(j, s):
                    cp.wait_send()


class Gather:
    TENSOR = (((), "xl", 0, 2048), ((), "core", 0, 2048), (("xl",), "core", 0, 2048))
    PAIR = (((), "xl", 0, 2048), ((), "y0", 0, 2048), ((), "core", 0, 2048),
            (("y0",), "xl", 0, 1024), (("xl",), "y0", 1024, 1024),
            (("y0",), "core", 0, 2048), (("xl",), "core", 0, 2048),
            (("xl", "y0"), "core", 0, 1024), (("xl", "y0"), "core", 1024, 1024))

    def __init__(self, me, full, sems, wide):
        self.me, self.full, self.sems, self.wide = me, full, sems, wide
        self.moves = self.PAIR if wide else self.TENSOR

    def copy(self, j, i):
        via, dim, col, width = self.moves[i]
        block = self.me
        for d in via:
            block = partner(block, d)
        view = self.full.at[own_rows(block, j, self.wide), pl.ds(col, width)]
        return remote(view, view, self.sems.at[j, i, 0], self.sems.at[j, i, 1], partner(self.me, dim))

    def start(self, j):
        for i in range(3 if self.wide else 2):
            self.copy(j, i).start()

    def relay(self, j):
        if not self.wide:
            self.copy(j, 0).wait_recv()
            self.copy(j, 2).start()
            return
        for came, onward in ((1, (3, 5)), (0, (4, 6)), (3, (7,)), (4, (8,))):
            self.copy(j, came).wait_recv()
            for i in onward:
                self.copy(j, i).start()

    def wait(self, j):
        for i in (2, 5, 6, 7, 8) if self.wide else (1, 2):
            self.copy(j, i).wait_recv()

    def finish(self):
        for j in range(2):
            for i in range(len(self.moves)):
                self.copy(j, i).wait_send()


def owner_runs(base, remaining):
    y, z, h, _ = base

    def ring(v, axis):
        both = (axis + "0" in remaining, axis + "1" in remaining)
        if all(both):
            return None
        if both[0]:
            return [v, flip4(v, "0")]
        if both[1]:
            return [v, flip4(v, "1")]
        return [v]

    ys, zs = ring(y, "y"), ring(z, "z")
    found = []
    for yy in [0, 1, 2, 3] if ys is None else ys:
        if zs is None and "xh" in remaining:
            found.append((yy * 512, 512))
            continue
        for zz in [0, 1, 2, 3] if zs is None else zs:
            if "xh" in remaining:
                found.append((yy * 512 + zz * 128, 128))
            else:
                found.append((yy * 512 + zz * 128 + h * 64, 64))
    return found


class Piece:
    def __init__(self, me, acc, order, keep, recvs, ssem, rsem, emit, stage=None, lsem=None):
        self.me, self.acc, self.order, self.keep, self.recvs = me, acc, order, keep, recvs
        self.ssem, self.rsem, self.emit, self.stage, self.lsem = ssem, rsem, emit, stage, lsem

    def rest(self, s):
        return self.order[s + 1:] + self.keep

    def send(self, s):
        to, off = partner(self.me, self.order[s]), 0
        for row, n in owner_runs(to, self.rest(s)):
            remote(self.acc(rows_at(row, n)), self.recvs[s].at[pl.ds(off, n)], self.ssem.at[s], self.rsem.at[s], to).start()
            off += n

    def arrived(self, s):
        wait_bytes(self.recvs[s], self.rsem.at[s])

    def load(self, s):
        return pltpu.make_async_copy(self.recvs[s], self.stage.at[pl.ds(0, 1024 >> s)], self.lsem)

    def add(self, s):
        view = self.recvs[s]
        if s < 2 and self.stage is not None:
            view = self.stage
        off = 0
        for i, (row, n) in enumerate(owner_runs(self.me, self.rest(s))):
            step = min(n, 128)

            def body(m, _, row=row, off=off, step=step, i=i):
                acc = self.acc(rows_at(row + m * step, step))
                v = acc[...].astype(F32) + view[pl.ds(pl.multiple_of(off + m * step, 64), step), :].astype(F32)
                if s == len(self.order) - 1:
                    self.emit(i, v)
                else:
                    acc[...] = v.astype(BF)
                return 0

            if n == step:
                body(0, 0)
            else:
                lax.fori_loop(0, n // step, body, 0)
            off += n
        if s < len(self.order) - 1:
            self.send(s + 1)

    def finish(self):
        for s in range(len(self.order)):
            wait_bytes(self.recvs[s], self.ssem.at[s])


def advance(pieces, s):
    if s < 2 and pieces[0].stage is not None:
        pieces[0].arrived(s)
        pieces[0].load(s).start()
        for i, piece in enumerate(pieces):
            if i + 1 < len(pieces):
                pieces[i + 1].arrived(s)
                pieces[i + 1].load(s).start()
            piece.load(s).wait()
            piece.add(s)
        return
    for piece in pieces:
        piece.arrived(s)
        piece.add(s)


class GainSum:
    def __init__(self, me, slots, sems):
        y, z, h, t = me
        self.axes = [(t, 4, lambda i: (y, z, h, i)),
                     (z * 2 + h, 8, lambda i: (y, i // 2, i % 2, t)),
                     (y, 4, lambda i: (i, z, h, t))]
        self.slots, self.sems = slots, sems

    def copies(self, s):
        here, n, place = self.axes[s]
        return [remote(self.slots[s].at[here], self.slots[s].at[here], self.sems[s].at[0, d], self.sems[s].at[1, d],
                       place((here + d) % n)) for d in range(1, n)]

    def start(self, s, value):
        self.slots[s][self.axes[s][0]] = value
        for cp in self.copies(s):
            cp.start()

    def take(self, s):
        for cp in self.copies(s):
            cp.wait_recv()
        total = self.slots[s][0]
        for i in range(1, self.axes[s][1]):
            total = total + self.slots[s][i]
        return total

    def finish(self):
        for s in range(3):
            for cp in self.copies(s):
                cp.wait_send()


class ContextSwap:
    def __init__(self, me, send, recv, sems):
        self.me, self.send, self.recv, self.sems = me, send, recv, sems
        self.ctx = me[1] * 2 + me[2]

    def copy(self, d):
        to = (self.ctx + d) % 8
        return remote(self.send.at[to], self.recv.at[self.ctx], self.sems.at[0, d], self.sems.at[1, d],
                      (self.me[0], to // 2, to % 2, self.me[3]))

    def start(self):
        for d in range(1, 8):
            self.copy(d).start()
        self.recv[self.ctx] = self.send[self.ctx]

    def wait(self):
        for d in range(1, 8):
            self.copy(d).wait_recv()

    def finish(self):
        for d in range(1, 8):
            self.copy(d).wait_send()


def rope_constants():
    frequency = np.float32(ROPE_BASE) ** (-np.arange(0, 128, 2).astype(np.float32) / np.float32(128))
    angles = np.arange(1024, dtype=np.float32)[:, None] * frequency.astype(np.float32)[None, :]
    cosine, sine = np.cos(angles), np.sin(angles)
    return (np.concatenate([cosine, cosine], 1).astype(np.float32),
            np.concatenate([-sine, sine], 1).astype(np.float32))


def half_turn(v):
    return pltpu.roll(v, 64, axis=1)


MLP_PIECES = ((0, 0, ("z0", "y1", "z1", "xh")), (0, 1, ("z1", "y1", "z0", "xh")),
              (1, 0, ("z0", "y1", "z1", "xh")), (1, 1, ("z1", "y1", "z0", "xh")),
              (0, 2, ("y1", "z0", "z1", "xh")), (1, 2, ("y1", "z1", "z0", "xh")),
              (2, 0, ("y1", "z0", "z1", "xh")), (2, 1, ("y1", "z1", "z0", "xh")),
              (2, 2, ("xh", "y1", "z0", "z1")))
OUT_ORDERS = (("y0", "z0", "z1", "y1", "xh"), ("y0", "z1", "z0", "y1", "xh"),
              ("y0", "y1", "z0", "z1", "xh"), ("y0", "z0", "y1", "z1", "xh"))
QKV_ORDERS = (("y0", "z0", "y1", "z1", "xh"), ("z0", "y1", "z1", "y0", "xh"),
              ("y1", "z1", "y0", "z0", "xh"), ("z1", "y0", "z0", "y1", "xh"))


def layer_kernel(x_h, g_h, gain1, gain2, qg, kg, wq_h, wk_h, wv_h, wo_h, wg_h, wu_h, wd_h, cos_h, sin_h,
                 block_ref, tok_ref, gains_ref, down_o, gate_o, up_o, out_o, q_o, k_o, v_o, p_h, mrecv0, mrecv1,
                 x, n1, n2, g2, wq, wk, wv, wo, wgt, wut, wdt, low_a, low_b, ra1, ra2, ra3, rb1, rb2, rb3, hidden,
                 qkv_s, qkv_r, mix_s, mix_r, gm_s, gm_r, dqkv_r, dkv, mix, proj, gqkv, mid_ref, gmid, x_own, cosv, sinv,
                 macc, mrecv2, mrecv3, stage, xsend, xrecv,
                 areca0, areca1, areca2, areca3, areca4, arecb0, arecb1, arecb2, arecb3, arecb4, gpart, gs0, gs1, gs2,
                 lsem, psem, s_qkv, s_mix, s_gm, s_dqkv, s_out, s_n2, s_gn2, s_feed, s_gb, s_blk, s_gn1, s_tok, g_sem,
                 mss, mrs, stsem, xs, ass, ars, bss, brs, gsem0, gsem1, gsem2):
    me = me_place()
    ctx = lax.axis_index("context")
    pair = pair_bit(me[0])
    half = pl.multiple_of(pair * 768, 256)

    def load(i, src, dst):
        return pltpu.make_async_copy(src, dst, lsem.at[i])

    first = [load(0, x_h, x), load(1, wk_h, wk), load(2, wv_h, wv),
             load(3, cos_h.at[rows_at(ctx * 128, 128)], cosv), load(4, sin_h.at[rows_at(ctx * 128, 128)], sinv),
             load(5, wq_h, wq), load(6, wo_h, wo)]
    homes = [rows_at(j * 256 + pair * 128, 128) for j in range(2)]
    first += [load(7 + j, g_h.at[pl.ds(j * 128, 128)], g2.at[homes[j]]) for j in range(2)]
    down_load = load(9, wd_h.at[pl.ds(half, 768)], wdt)
    tiles = []
    for i in range(3):
        c = pl.ds(pl.multiple_of(half + i * 256, 256), 256)
        tiles.append((load(10 + i, wg_h.at[:, c], wgt.at[i]), load(13 + i, wu_h.at[:, c], wut.at[i])))
    for cp in first:
        cp.start()
    bar = pltpu.get_barrier_semaphore()
    for d in range(1, 8):
        pl.semaphore_signal(bar, inc=1, device_id=(me[0], (ctx + d) % 8, me[3]), device_id_type=MESH)
    for d in range(1, 4):
        pl.semaphore_signal(bar, inc=1, device_id=(me[0], ctx, (me[3] + d) % 4), device_id_type=MESH)
        pl.semaphore_signal(bar, inc=1, device_id=((me[0] + d) % 4, ctx, me[3]), device_id_type=MESH)

    first[0].wait()
    g1 = row_of(gain1)

    def norm_rows(i, _):
        r = pl.ds(pl.multiple_of(i * 32, 32), 32)
        xv = x[r, :].astype(F32)
        inv = lax.rsqrt(jnp.mean(xv * xv, axis=-1, keepdims=True) + EPSILON)
        n1[r, :] = (xv * inv * g1).astype(BF)
        return 0

    lax.fori_loop(0, 8, norm_rows, 0)
    for j in range(2):
        x_own[j * 32:(j + 1) * 32, :] = x[own_rows(me, j, False), :]
    for i in (1, 2, 3, 4):
        first[i].wait()
    cos2 = jnp.concatenate([cosv[...], cosv[...]], axis=0)
    sin2 = jnp.concatenate([sinv[...], sinv[...]], axis=0)
    gqf, gkf = row_of(qg), row_of(kg)

    def turned(v, gain):
        hat = v * lax.rsqrt(jnp.mean(v * v, axis=-1, keepdims=True) + EPSILON) * gain
        return (hat * cos2 + half_turn(hat) * sin2).astype(BF)

    def spread(first, width, heads, value):
        for s in range(2):
            for h in range(4):
                c = h * width // 4 * 128
                qkv_s[s * 4 + h, :, first:first + 128] = value[s * 128:(s + 1) * 128, c:c + 128]

    kp = dot(n1[...], wk[...])
    proj[:, 512:768] = kp
    spread(128, 2, 2, jnp.concatenate([turned(kp[:, h * 128:(h + 1) * 128], gkf) for h in range(2)], axis=1))
    spread(256, 2, 2, dot(n1[...], wv[...]).astype(BF))
    first[5].wait()
    qp = dot(n1[...], wq[...])
    proj[:, 0:512] = qp
    spread(0, 4, 4, jnp.concatenate([turned(qp[:, h * 128:(h + 1) * 128], gqf) for h in range(4)], axis=1))
    pl.semaphore_wait(bar, 13)
    swap_qkv = ContextSwap(me, qkv_s, qkv_r, s_qkv)
    swap_qkv.start()
    g_copies = [remote(g2.at[homes[j]], g2.at[homes[j]], g_sem.at[0, j], g_sem.at[1, j], partner(me, "y0")) for j in range(2)]
    for j in range(2):
        first[7 + j].wait()
        g_copies[j].start()
    down_load.start()
    for pair_loads in tiles:
        for cp in pair_loads:
            cp.start()
    first[6].wait()
    swap_qkv.wait()

    def part(ref, n, first):
        return ref[0:n * 2, :, first:first + 128].reshape(n * 256, 128)

    def prob_home(i, j):
        n = i * 4 + j
        return (n // 2, slice((n % 2) * 256, (n % 2 + 1) * 256))

    seen = lax.broadcasted_iota(jnp.int32, (256, 256), 0) >= lax.broadcasted_iota(jnp.int32, (256, 256), 1)
    for i in range(4):
        q = qkv_r[2 * i:2 * i + 2, :, 0:128].reshape(256, 128)
        scores = dot_nt(q, part(qkv_r, i + 1, 128)) * SCALE
        last = jnp.where(seen, scores[:, i * 256:], -1e30)
        scores = last if i == 0 else jnp.concatenate([scores[:, :i * 256], last], axis=1)
        e = jnp.exp(scores - jnp.max(scores, axis=-1, keepdims=True))
        prob = (e / jnp.sum(e, axis=-1, keepdims=True)).astype(BF)
        for j in range(i + 1):
            hidden[prob_home(i, j)] = prob[:, j * 256:(j + 1) * 256]
        mix_s[2 * i:2 * i + 2] = dot(prob, part(qkv_r, i + 1, 256)).astype(BF).reshape(2, 128, 128)
    swap_mix = ContextSwap(me, mix_s, mix_r, s_mix)
    swap_mix.start()
    p_out = pltpu.make_async_copy(hidden.at[pl.ds(0, 8)], p_h, psem.at[0])
    p_out.start()
    for cp in g_copies:
        cp.wait_recv()
    down_load.wait()
    swap_mix.wait()
    for p in range(8):
        mix[(p // 4) * 128:(p // 4 + 1) * 128, (p % 4) * 128:(p % 4 + 1) * 128] = mix_r[p]

    sum_o = GroupSum(me, low_a.at[0:256], (ra1, ra2), s_out, False)
    for j in range(2):
        low_a[j * 128:(j + 1) * 128, :] = dot(mix[j * 128:(j + 1) * 128, :], wo[...]).astype(BF)
        sum_o.send(j)
    p_out.wait()
    for i in range(3):
        hidden[6 + i] = dot_nt(g2[...], wdt[i * 256:(i + 1) * 256, :]).astype(BF)
    for j in range(2):
        sum_o.step(j, 0)
    gather_n = Gather(me, n2, s_n2, True)
    scale2 = row_of(gain2)

    def halves(j):
        return slice(j * 32, (j + 1) * 32)

    for j in range(2):
        mid = x_own[halves(j), :].astype(F32) + sum_o.step(j, 1)
        mid_ref[halves(j), :] = mid
        inv = lax.rsqrt(jnp.mean(mid * mid, axis=-1, keepdims=True) + EPSILON)
        n2[own_rows(me, j, True), :] = (mid * inv * scale2).astype(BF)
        gather_n.start(j)
    for i in range(3):
        for cp in tiles[i]:
            cp.wait()
    sum_o.finish()
    sum2 = GroupSum(me, low_a, (ra1, ra2, ra3), s_gn2, True)
    sumf = GroupSum(me, low_b, (rb1, rb2, rb3), s_feed, True)
    for j in range(2):
        gather_n.relay(j)
    for j in range(2):
        gather_n.wait(j)
        r = slice(j * 256, (j + 1) * 256)
        for i in range(3):
            gate = dot(n2[r, :], wgt[i])
            up = dot(n2[r, :], wut[i])
            gh = hidden[6 + i, r, :].astype(F32)
            sig = 1.0 / (1.0 + jnp.exp(-gate))
            silu = gate * sig
            hidden[i, r, :] = (silu * up).astype(BF)
            hidden[3 + i, r, :] = (gh * up * sig * (1.0 + gate * (1.0 - sig))).astype(BF)
            hidden[6 + i, r, :] = (gh * silu).astype(BF)
        for n in range(4):
            c = slice(n * 512, (n + 1) * 512)
            v = dot_nt(hidden[3, r, :], wgt[0, c, :]) + dot_nt(hidden[6, r, :], wut[0, c, :])
            for i in (1, 2):
                v = v + dot_nt(hidden[3 + i, r, :], wgt[i, c, :]) + dot_nt(hidden[6 + i, r, :], wut[i, c, :])
            low_a[r, c] = v.astype(BF)
        sum2.send(j)

    mlp, slot = [], {}
    for n, (k, i, dims) in enumerate(MLP_PIECES):
        slot[k, i] = n
        out = (down_o, gate_o, up_o)[k]

        def emit(m, v, out=out, i=i, n=n):
            if m == 0:
                out[pair, :, i * 256:(i + 1) * 256] = v
            else:
                xsend[n] = v.astype(BF)

        mlp.append(Piece(me, lambda r, n=n: macc.at[n, r], dims, ("y0",),
                         (mrecv0.at[n], mrecv1.at[n], mrecv2.at[n], mrecv3.at[n]), mss.at[n], mrs.at[n], emit,
                         stage.at[n % 2], stsem.at[n % 2]))
    four = range(4)

    def outer(left, k, c):
        t = left[:, c].T
        for weight in k:
            for i in range(3):
                macc[slot[weight, i], c, :] = dot(t, hidden[weight * 3 + i]).astype(BF)

    for n in four:
        outer(g2, (0,), slice(n * 512, (n + 1) * 512))
        if n % 2:
            sum2.step(n // 2, 0)
    for piece in (mlp[0], mlp[1], mlp[4]):
        piece.send(0)
    for n in four:
        outer(n2, (1, 2), slice(n * 512, (n + 1) * 512))
        if n % 2:
            sum2.step(n // 2, 1)
    for piece in mlp[2:4] + mlp[5:8]:
        piece.send(0)
    p_in = pltpu.make_async_copy(p_h, hidden.at[pl.ds(0, 8)], psem.at[1])
    for n in four:
        c = slice(n * 512, (n + 1) * 512)
        v = dot(hidden[0], wdt[0:256, c])
        for i in (1, 2):
            v = v + dot(hidden[i], wdt[i * 256:(i + 1) * 256, c])
        low_b[:, c] = v.astype(BF)
    p_in.start()

    gb = x
    gather_b = Gather(me, gb, s_gb, False)
    gain_term = jnp.zeros((1, 2048), F32)
    for j in range(2):
        mid = mid_ref[halves(j), :]
        inv = lax.rsqrt(jnp.mean(mid * mid, axis=-1, keepdims=True) + EPSILON)
        hat = mid * inv
        grad = sum2.step(j, 2)
        gain_term = gain_term + jnp.sum(grad * hat, axis=0, keepdims=True)
        u = grad * scale2
        grad = g2[own_rows(me, j, True), :].astype(F32) + inv * (u - hat * jnp.mean(u * hat, axis=-1, keepdims=True))
        gmid[halves(j), :] = grad
        gb[own_rows(me, j, False), :] = grad.astype(BF)
        gather_b.start(j)
    gpart[...] = jnp.zeros((40, 128), F32)

    def put_gain(row, value):
        for i in range(value.shape[1] // 128):
            gpart[row + i:row + i + 1, :] = value[:, i * 128:(i + 1) * 128]

    put_gain(16, gain_term)
    for j in range(2):
        gather_b.relay(j)
    for j in range(2):
        gather_b.wait(j)

    for b in range(2):
        gmix = dot_nt(gb[...], wo[b * 256:(b + 1) * 256, :]).astype(BF)
        for s in range(2):
            for h in range(2):
                gm_s[s * 4 + b * 2 + h] = gmix[s * 128:(s + 1) * 128, h * 128:(h + 1) * 128]
    swap_gm = ContextSwap(me, gm_s, gm_r, s_gm)
    swap_gm.start()
    for j in range(2):
        sumf.send(j)
    mlp[8].send(0)

    att_a, att_b = [], []
    spots = [(lambda r, i=i: wut.at[1 + i // 2, r, pl.ds((i % 2) * 128, 128)]) for i in range(4)]
    spots += [(lambda r, i=i: (wgt.at[i, r] if i < 3 else wut.at[0, r])) for i in range(4)]
    for i in range(4):
        def emit_a(m, v, i=i):
            out_o[:, i * 128:(i + 1) * 128] = v

        def emit_b(m, v, i=i):
            (q_o, q_o, k_o, v_o)[i][:, (i * 256 if i == 1 else 0):(i * 256 if i == 1 else 0) + 256] = v

        att_a.append(Piece(me, spots[i], OUT_ORDERS[i], (), tuple(r.at[i] for r in (areca0, areca1, areca2, areca3, areca4)),
                           ass.at[i], ars.at[i], emit_a))
        att_b.append(Piece(me, spots[4 + i], QKV_ORDERS[i], (), tuple(r.at[i] for r in (arecb0, arecb1, arecb2, arecb3, arecb4)),
                           bss.at[i], brs.at[i], emit_b))
    for j in four:
        c = slice(j * 512, (j + 1) * 512)
        v = dot(gb[:, c].T, mix[...]).astype(BF)
        wut[1, c, :] = v[:, 0:256]
        wut[2, c, :] = v[:, 256:512]
    for j in range(2):
        sumf.step(j, 0)
    for piece in att_a:
        piece.send(0)
    p_in.wait()
    swap_qkv.finish()
    swap_gm.wait()
    for i in range(4):
        n = (i + 1) * 256
        gm = gm_r[2 * i:2 * i + 2].reshape(256, 128)
        prob = jnp.concatenate([hidden[prob_home(i, j)] for j in range(i + 1)], axis=1)
        gp = dot_nt(gm, part(qkv_r, i + 1, 256))
        prob32 = prob.astype(F32)
        gs = (prob32 * (gp - jnp.sum(prob32 * gp, axis=-1, keepdims=True))).astype(BF)
        q = qkv_r[2 * i:2 * i + 2, :, 0:128].reshape(256, 128)
        qkv_s[2 * i:2 * i + 2, :, 0:128] = (dot(gs, part(qkv_r, i + 1, 128)) * SCALE).astype(BF).reshape(2, 128, 128)
        gk = dot_tn(gs, q)
        gv = dot_tn(prob, gm)
        if i:
            dkv[0:n - 256, 0:128] += gk[0:n - 256]
            dkv[0:n - 256, 128:256] += gv[0:n - 256]
        dkv[n - 256:n, 0:128] = gk[n - 256:n]
        dkv[n - 256:n, 128:256] = gv[n - 256:n]
    qkv_s[:, :, 128:256] = (dkv[:, 0:128] * SCALE).astype(BF).reshape(8, 128, 128)
    qkv_s[:, :, 256:384] = dkv[:, 128:256].astype(BF).reshape(8, 128, 128)
    swap_dqkv = ContextSwap(me, qkv_s, dqkv_r, s_dqkv)
    swap_dqkv.start()
    for j in range(2):
        sumf.step(j, 1)
    advance(mlp[0:4], 0)
    gather_o = Gather(me, block_ref, s_blk, False)
    for j in range(2):
        block_ref[own_rows(me, j, False), :] = (mid_ref[halves(j), :] + sumf.step(j, 2)).astype(BF)
        gather_o.start(j)
    advance(mlp[4:6], 0)

    def through_norm(grad_rot, pre, gain):
        grad_normed = grad_rot * cos2 - half_turn(grad_rot) * sin2
        inv = lax.rsqrt(jnp.mean(pre * pre, axis=-1, keepdims=True) + EPSILON)
        hat = pre * inv
        u = grad_normed * gain
        grad_pre = inv * (u - hat * jnp.mean(u * hat, axis=-1, keepdims=True))
        return grad_pre.astype(BF), jnp.sum(grad_normed * hat, axis=0, keepdims=True)

    def arrived(first, heads):
        rows = []
        for s in range(2):
            v = dqkv_r[s * 4 + heads[0], :, first:first + 128].astype(F32)
            for h in heads[1:]:
                v = v + dqkv_r[s * 4 + h, :, first:first + 128].astype(F32)
            rows.append(v)
        return jnp.concatenate(rows, axis=0)

    swap_dqkv.wait()
    gain_sum = jnp.zeros((1, 128), F32)
    for h in range(4):
        c = slice(h * 128, (h + 1) * 128)
        gqkv[:, c], term = through_norm(arrived(0, (h,)), proj[:, c], gqf)
        gain_sum = gain_sum + term
    put_gain(32, gain_sum)
    gain_sum = jnp.zeros((1, 128), F32)
    for h in range(2):
        c = slice(512 + h * 128, 640 + h * 128)
        gqkv[:, c], term = through_norm(arrived(128, (2 * h, 2 * h + 1)), proj[:, c], gkf)
        gain_sum = gain_sum + term
        gqkv[:, 768 + h * 128:896 + h * 128] = arrived(256, (2 * h, 2 * h + 1)).astype(BF)
    put_gain(33, gain_sum)

    sum2.finish()
    sum1 = GroupSum(me, low_a.at[0:256], (ra1, ra2), s_gn1, False)
    for j in range(2):
        r = slice(j * 128, (j + 1) * 128)
        v = dot_nt(gqkv[r, 0:512], wq[...]) + dot_nt(gqkv[r, 512:768], wk[...]) + dot_nt(gqkv[r, 768:1024], wv[...])
        low_a[r, :] = v.astype(BF)
        sum1.send(j)
    for n in four:
        c = slice(n * 512, (n + 1) * 512)
        v = dot(n1[:, c].T, gqkv[...]).astype(BF)
        for i in range(3):
            wgt[i, c, :] = v[:, i * 256:(i + 1) * 256]
        wut[0, c, :] = v[:, 768:1024]
    for piece in att_b:
        piece.send(0)
    for j in range(2):
        sum1.step(j, 0)
    for j in range(2):
        gather_o.relay(j)
    scale1 = row_of(gain1)
    gather_t = Gather(me, tok_ref, s_tok, False)
    gain_term = jnp.zeros((1, 2048), F32)
    for j in range(2):
        xo = x_own[halves(j), :].astype(F32)
        inv = lax.rsqrt(jnp.mean(xo * xo, axis=-1, keepdims=True) + EPSILON)
        hat = xo * inv
        grad = sum1.step(j, 1)
        gain_term = gain_term + jnp.sum(grad * hat, axis=0, keepdims=True)
        u = grad * scale1
        tok_ref[own_rows(me, j, False), :] = (
            gmid[halves(j), :] + inv * (u - hat * jnp.mean(u * hat, axis=-1, keepdims=True))).astype(BF)
        gather_t.start(j)
    put_gain(0, gain_term)
    gains = GainSum(me, (gs0, gs1, gs2), (gsem0, gsem1, gsem2))
    gains.start(0, gpart[...])
    advance(mlp[6:8], 0)
    advance(mlp[8:9], 0)
    advance(mlp[0:4], 1)
    gains.start(1, gains.take(0))
    for j in range(2):
        gather_t.relay(j)
    advance(att_a, 0)
    advance(mlp[4:8], 1)
    advance(att_b, 0)
    gains.start(2, gains.take(1))
    advance(mlp[8:9], 1)
    advance(att_a, 1)
    advance(mlp, 2)
    advance(att_b, 1)
    advance(mlp, 3)
    swap = [remote(xsend.at[n], xrecv.at[n], xs.at[n, 0], xs.at[n, 1], partner(me, "y0")) for n in range(9)]
    for cp in swap:
        cp.start()
    advance(att_a, 2)
    gains_ref[...] = gains.take(2)
    advance(att_b, 2)
    advance(att_a, 3)
    advance(att_b, 3)
    advance(att_a, 4)
    advance(att_b, 4)
    for n, cp in enumerate(swap):
        cp.wait_recv()
        k, i, _ = MLP_PIECES[n]
        (down_o, gate_o, up_o)[k][1 - pair, :, i * 256:(i + 1) * 256] = xrecv[n].astype(F32)

    for cp in swap:
        cp.wait_send()
    for gather in (gather_b, gather_o, gather_t):
        gather.finish()
    for gather in (gather_o, gather_t):
        for j in range(2):
            gather.wait(j)
    gather_n.finish()
    gains.finish()
    sum1.finish()
    for cp in g_copies:
        cp.wait_send()
    swap_mix.finish()
    swap_gm.finish()
    swap_dqkv.finish()
    sumf.finish()
    for piece in mlp + att_a + att_b:
        piece.finish()


def layer(x, g, gain1, gain2, qg, kg, wq, wk, wv, wo, wg, wu, wd):
    cos_t, sin_t = rope_constants()
    V = pl.BlockSpec(memory_space=pltpu.VMEM)
    A = pl.BlockSpec(memory_space=pl.ANY)
    S = jax.ShapeDtypeStruct
    D = pltpu.SemaphoreType.DMA
    M = pltpu.VMEM
    return pl.pallas_call(
        layer_kernel,
        out_shape=(S((256, 2048), BF), S((256, 2048), BF), S((40, 128), F32),
                   S((2, 64, 768), F32), S((2, 64, 768), F32), S((2, 64, 768), F32), S((64, 512), F32), S((64, 512), F32),
                   S((64, 256), F32), S((64, 256), F32), S((8, 512, 256), BF), S((9, 1024, 256), BF), S((9, 512, 256), BF)),
        in_specs=[A, A, V, V, V, V] + [A] * 9,
        out_specs=(V,) * 10 + (A, A, A),
        scratch_shapes=[
            M((256, 2048), BF), M((256, 2048), BF), M((512, 2048), BF), M((512, 2048), BF),
            M((2048, 512), BF), M((2048, 256), BF), M((2048, 256), BF), M((512, 2048), BF),
            M((3, 2048, 256), BF), M((3, 2048, 256), BF), M((768, 2048), BF),
            M((512, 2048), BF), M((512, 2048), BF),
            M((2, 4, 32, 2048), BF), M((2, 2, 32, 2048), BF), M((2, 1, 32, 2048), BF),
            M((2, 4, 32, 2048), BF), M((2, 2, 32, 2048), BF), M((2, 1, 32, 2048), BF), M((9, 512, 256), BF),
            M((8, 128, 384), BF), M((8, 128, 384), BF), M((8, 128, 128), BF), M((8, 128, 128), BF), M((8, 128, 128), BF),
            M((8, 128, 128), BF), M((8, 128, 384), BF), M((1024, 256), F32), M((256, 512), BF), M((256, 768), F32),
            M((256, 1024), BF), M((64, 2048), F32), M((64, 2048), F32),
            M((64, 2048), BF), M((128, 128), F32), M((128, 128), F32),
            M((9, 2048, 256), BF), M((9, 256, 256), BF), M((9, 128, 256), BF),
            M((2, 1024, 256), BF), M((9, 64, 256), BF), M((9, 64, 256), BF)]
        + [M((4, 1024 >> s, 128), BF) for s in range(5)] + [M((4, 1024 >> s, 256), BF) for s in range(5)]
        + [M((40, 128), F32), M((4, 40, 128), F32), M((8, 40, 128), F32), M((4, 40, 128), F32),
           D((16,)), D((2,)), D((2, 8)), D((2, 8)), D((2, 8)), D((2, 8)), D((2, 2, 2, 2)), D((2, 9, 2)), D((3, 2, 4, 2)),
           D((3, 2, 4, 2)), D((2, 3, 2)), D((2, 3, 2)), D((2, 2, 2, 2)), D((2, 3, 2)), D((2, 2)),
           D((9, 4)), D((9, 4)), D((2,)), D((9, 2)), D((4, 5)), D((4, 5)), D((4, 5)), D((4, 5)),
           D((2, 4)), D((2, 8)), D((2, 4))],
        compiler_params=pltpu.CompilerParams(collective_id=3, has_side_effects=True, vmem_limit_bytes=63 * 2**20),
    )(x, g, gain1, gain2, qg, kg, wq, wk, wv, wo, wg, wu, wd, jnp.asarray(cos_t), jnp.asarray(sin_t))


def tail_kernel(block_h, tok_h, gains, down_h, gate_h, up_h, out_h, q_h, k_h, v_h,
                block_o, tok_o, gain1_o, q_o, k_o, v_o, qg_o, kg_o, out_o, gain2_o, gate_o, up_o, down_o, sems):
    pairs = [(block_h, block_o), (tok_h, tok_o), (q_h, q_o), (k_h, k_o), (v_h, v_o), (out_h, out_o)]
    for i in range(2):
        c = pl.ds(i * 768, 768)
        pairs += [(down_h.at[i], down_o.at[:, c]), (gate_h.at[i], gate_o.at[:, c]), (up_h.at[i], up_o.at[:, c])]
    copies = [pltpu.make_async_copy(s, d, sems.at[i]) for i, (s, d) in enumerate(pairs)]
    for cp in copies:
        cp.start()
    gain1_o[...] = gains[0:16]
    gain2_o[...] = gains[16:32]
    qg_o[...] = gains[32:33]
    kg_o[...] = gains[33:34]
    for cp in copies:
        cp.wait()


def tail(block, tok, gains, down, gate, up, out, q, k, v):
    V = pl.BlockSpec(memory_space=pltpu.VMEM)
    A = pl.BlockSpec(memory_space=pl.ANY)
    S = jax.ShapeDtypeStruct
    return pl.pallas_call(
        tail_kernel,
        out_shape=(S((256, 2048), BF), S((256, 2048), BF), S((16, 128), F32), S((64, 512), F32), S((64, 256), F32),
                   S((64, 256), F32), S((1, 128), F32), S((1, 128), F32), S((64, 512), F32), S((16, 128), F32),
                   S((64, 1536), F32), S((64, 1536), F32), S((64, 1536), F32)),
        in_specs=[A, A, V, A, A, A, A, A, A, A],
        out_specs=(V,) * 13,
        scratch_shapes=[pltpu.SemaphoreType.DMA((12,))],
        compiler_params=pltpu.CompilerParams(vmem_limit_bytes=62 * 2**20),
    )(block, tok, gains, down, gate, up, out, q, k, v)


def local(tokens, attn_gain, w_query, w_key, w_value, query_gain, key_gain, w_out, mlp_gain, w_gate, w_up, w_down, out_grad):
    results = layer(tokens.reshape(256, 2048), out_grad.reshape(256, 2048), attn_gain, mlp_gain, query_gain, key_gain,
                    w_query, w_key, w_value, w_out, w_gate, w_up, w_down)
    block, tok, g1, q, k, v, qg, kg, out, g2, gate, up, down = tail(*results[:10])
    return (block.reshape(2, 128, 2048), tok.reshape(2, 128, 2048), g1.reshape(2048), q, k, v, qg.reshape(128),
            kg.reshape(128), out.T, g2.reshape(2048), gate, up, down.T)


def solution(mesh):
    in_specs = (
        P("dp", "context", None),
        P(),
        P(None, "tensor"),
        P(None, "tensor"),
        P(None, "tensor"),
        P(),
        P(),
        P("tensor", None),
        P(),
        P(None, "tensor"),
        P(None, "tensor"),
        P("tensor", None),
        P("dp", "context", None),
    )
    out_specs = (
        P("dp", "context", None),
        P("dp", "context", None),
        P(),
        P(("dp", "context"), "tensor"),
        P(("dp", "context"), "tensor"),
        P(("dp", "context"), "tensor"),
        P(),
        P(),
        P("tensor", ("dp", "context")),
        P(),
        P(("dp", "context"), "tensor"),
        P(("dp", "context"), "tensor"),
        P("tensor", ("dp", "context")),
    )
    return jax.shard_map(local, mesh=mesh, in_specs=in_specs, out_specs=out_specs, check_vma=False)
```

profile of v0, /device:TPU:0, one launch (start us, length us, event | category | flops | bytes accessed | tf_op | source)
XLA Modules:
  0.0 199.5 jit_solution(14791366891898848017)
XLA Ops:
  0.6 194.0 %shard_map.246 = (bf16[256,2048]{1,0:T(8,128)(2,1)}, bf16[256,2048]{1,0:T(8,128)(2,1)}, f32[40,128]{1,0:T(8,128)}, f32[2,64,768]{2,1,0:T(8,128)}, f32[2,64,768]{...) custom-call(bf16[256,2048]{1,0:T(8,128)(2,1)} %bitcast.10, ...), custom_call_target="tpu_custom_call" | custom-call | tf_op jit(solution)/shard_map/pallas_call | solution.py:766
  194.7 4.7 %shard_map.247 = (bf16[256,2048]{1,0:T(8,128)(2,1)}, bf16[256,2048]{1,0:T(8,128)(2,1)}, f32[16,128]{1,0:T(8,128)}, f32[64,512]{1,0:T(8,128)}, f32[64,256]{1,0:T(...) custom-call(bf16[256,2048]{1,0:T(8,128)(2,1)} %get-tuple-element.36., ...), custom_call_target="tpu_custom_call" | custom-call | tf_op jit(solution)/shard_map/pallas_call | solution.py:817
where the time goes:
time: 200 us
  Pallas kernels  199 us (100%)
    pallas_call x1, Pallas kernels, layer(): pl.pallas_call(layer_kernel, out_shape=(S((256, 2048), BF), S((256, 2048)...  194 us
    pallas_call x1, Pallas kernels, tail(): pl.pallas_call(tail_kernel, out_shape=(S((256, 2048), BF), S((256, 2048),...  4.66 us

commit v1 on v0

--- a/solution.py
+++ b/solution.py
@@ -168,31 +168,12 @@
                 self.copy(j, i).wait_send()
 
 
-def owner_runs(base, remaining):
-    y, z, h, _ = base
-
-    def ring(v, axis):
-        both = (axis + "0" in remaining, axis + "1" in remaining)
-        if all(both):
-            return None
-        if both[0]:
-            return [v, flip4(v, "0")]
-        if both[1]:
-            return [v, flip4(v, "1")]
-        return [v]
-
-    ys, zs = ring(y, "y"), ring(z, "z")
-    found = []
-    for yy in [0, 1, 2, 3] if ys is None else ys:
-        if zs is None and "xh" in remaining:
-            found.append((yy * 512, 512))
-            continue
-        for zz in [0, 1, 2, 3] if zs is None else zs:
-            if "xh" in remaining:
-                found.append((yy * 512 + zz * 128, 128))
-            else:
-                found.append((yy * 512 + zz * 128 + h * 64, 64))
-    return found
+def dim_bit(place, dim):
+    y, z, h, _ = place
+    if dim == "xh":
+        return h
+    v = y if dim[0] == "y" else z
+    return pair_bit(v) if dim[1] == "0" else v // 2
 
 
 class Piece:
@@ -200,45 +181,50 @@
         self.me, self.acc, self.order, self.keep, self.recvs = me, acc, order, keep, recvs
         self.ssem, self.rsem, self.emit, self.stage, self.lsem = ssem, rsem, emit, stage, lsem
 
-    def rest(self, s):
-        return self.order[s + 1:] + self.keep
+    def put(self, y, value):
+        dims = self.order + self.keep
+        for z in range(4):
+            for h in range(2):
+                spot = 0
+                for i, dim in enumerate(dims):
+                    here = dim_bit(self.me, dim)
+                    spot = spot + (1 - here if dim_bit((y, z, h, 0), dim) else here) * (1024 >> i)
+                b = (z * 2 + h) * 64
+                self.acc(rows_at(spot, 64))[...] = value[b:b + 64]
 
     def send(self, s):
-        to, off = partner(self.me, self.order[s]), 0
-        for row, n in owner_runs(to, self.rest(s)):
-            remote(self.acc(rows_at(row, n)), self.recvs[s].at[pl.ds(off, n)], self.ssem.at[s], self.rsem.at[s], to).start()
-            off += n
+        n = 1024 >> s
+        remote(self.acc(pl.ds(n, n)), self.recvs[s], self.ssem.at[s], self.rsem.at[s], partner(self.me, self.order[s])).start()
 
     def arrived(self, s):
         wait_bytes(self.recvs[s], self.rsem.at[s])
 
-    def load(self, s):
-        return pltpu.make_async_copy(self.recvs[s], self.stage.at[pl.ds(0, 1024 >> s)], self.lsem)
+    def loads(self):
+        return [pltpu.make_async_copy(self.recvs[0].at[pl.ds(i * 512, 512)], self.stage[i], self.lsem.at[i]) for i in range(2)]
 
     def add(self, s):
-        view = self.recvs[s]
-        if s < 2 and self.stage is not None:
-            view = self.stage
-        off = 0
-        for i, (row, n) in enumerate(owner_runs(self.me, self.rest(s))):
-            step = min(n, 128)
-
-            def body(m, _, row=row, off=off, step=step, i=i):
-                acc = self.acc(rows_at(row + m * step, step))
-                v = acc[...].astype(F32) + view[pl.ds(pl.multiple_of(off + m * step, 64), step), :].astype(F32)
-                if s == len(self.order) - 1:
-                    self.emit(i, v)
-                else:
-                    acc[...] = v.astype(BF)
+        n = 1024 >> s
+        if s == len(self.order) - 1:
+            v = self.acc(pl.ds(0, n))[...].astype(F32) + self.recvs[s][...].astype(F32)
+            for i in range(n // 64):
+                self.emit(i, v[i * 64:(i + 1) * 64])
+            return
+        parts = [(0, n, self.recvs[s])]
+        if s == 0 and self.stage is not None:
+            parts = [(0, 512, self.stage[0]), (512, 512, self.stage[1])]
+        for first, count, view in parts:
+            step = min(count, 128)
+
+            def body(m, _, first=first, step=step, view=view):
+                acc = self.acc(rows_at(first + m * step, step))
+                acc[...] = (acc[...].astype(F32) + view[rows_at(m * step, step), :].astype(F32)).astype(BF)
                 return 0
 
-            if n == step:
+            if count == step:
                 body(0, 0)
             else:
-                lax.fori_loop(0, n // step, body, 0)
-            off += n
-        if s < len(self.order) - 1:
-            self.send(s + 1)
+                lax.fori_loop(0, count // step, body, 0)
+        self.send(s + 1)
 
     def finish(self):
         for s in range(len(self.order)):
@@ -246,19 +232,24 @@
 
 
 def advance(pieces, s):
-    if s < 2 and pieces[0].stage is not None:
-        pieces[0].arrived(s)
-        pieces[0].load(s).start()
-        for i, piece in enumerate(pieces):
-            if i + 1 < len(pieces):
-                pieces[i + 1].arrived(s)
-                pieces[i + 1].load(s).start()
-            piece.load(s).wait()
+    if s or pieces[0].stage is None:
+        for piece in pieces:
+            piece.arrived(s)
             piece.add(s)
         return
-    for piece in pieces:
-        piece.arrived(s)
-        piece.add(s)
+
+    def fetch(piece):
+        piece.arrived(0)
+        for cp in piece.loads():
+            cp.start()
+
+    fetch(pieces[0])
+    for i, piece in enumerate(pieces):
+        if i + 1 < len(pieces):
+            fetch(pieces[i + 1])
+        for cp in piece.loads():
+            cp.wait()
+        piece.add(0)
 
 
 class GainSum:
@@ -329,22 +320,22 @@
     return pltpu.roll(v, 64, axis=1)
 
 
-MLP_PIECES = ((0, 0, ("z0", "y1", "z1", "xh")), (0, 1, ("z1", "y1", "z0", "xh")),
-              (1, 0, ("z0", "y1", "z1", "xh")), (1, 1, ("z1", "y1", "z0", "xh")),
-              (0, 2, ("y1", "z0", "z1", "xh")), (1, 2, ("y1", "z1", "z0", "xh")),
-              (2, 0, ("y1", "z0", "z1", "xh")), (2, 1, ("y1", "z1", "z0", "xh")),
-              (2, 2, ("xh", "y1", "z0", "z1")))
+MLP_PIECES = ((0, 0, ("z0", "z1", "xh", "y1")), (0, 1, ("z1", "z0", "xh", "y1")),
+              (1, 0, ("z0", "z1", "xh", "y1")), (1, 1, ("z1", "z0", "xh", "y1")),
+              (0, 2, ("y1", "xh", "z0", "z1")), (1, 2, ("y1", "xh", "z1", "z0")),
+              (2, 0, ("y1", "xh", "z0", "z1")), (2, 1, ("y1", "xh", "z1", "z0")),
+              (2, 2, ("y1", "xh", "z0", "z1")))
 OUT_ORDERS = (("y0", "z0", "z1", "y1", "xh"), ("y0", "z1", "z0", "y1", "xh"),
-              ("y0", "y1", "z0", "z1", "xh"), ("y0", "z0", "y1", "z1", "xh"))
-QKV_ORDERS = (("y0", "z0", "y1", "z1", "xh"), ("z0", "y1", "z1", "y0", "xh"),
-              ("y1", "z1", "y0", "z0", "xh"), ("z1", "y0", "z0", "y1", "xh"))
+              ("y0", "z0", "y1", "z1", "xh"), ("y0", "z1", "y1", "z0", "xh"))
+QKV_ORDERS = (("y0", "y1", "z0", "z1", "xh"), ("y1", "y0", "z1", "z0", "xh"),
+              ("z0", "z1", "y0", "y1", "xh"), ("z1", "z0", "y1", "y0", "xh"))
 
 
 def layer_kernel(x_h, g_h, gain1, gain2, qg, kg, wq_h, wk_h, wv_h, wo_h, wg_h, wu_h, wd_h, cos_h, sin_h,
-                 block_ref, tok_ref, gains_ref, down_o, gate_o, up_o, out_o, q_o, k_o, v_o, p_h, mrecv0, mrecv1,
+                 block_ref, tok_ref, gains_ref, down_o, gate_o, up_o, out_o, q_o, k_o, v_o, p_h, mrecv0,
                  x, n1, n2, g2, wq, wk, wv, wo, wgt, wut, wdt, low_a, low_b, ra1, ra2, ra3, rb1, rb2, rb3, hidden,
-                 qkv_s, qkv_r, mix_s, mix_r, gm_s, gm_r, dqkv_r, dkv, mix, proj, gqkv, mid_ref, gmid, x_own, cosv, sinv,
-                 macc, mrecv2, mrecv3, stage, xsend, xrecv,
+                 qkv_s, qkv_r, mix_s, mix_r, gm_r, dqkv_r, dkv, mix, proj, gqkv, mid_ref, gmid, x_own, cosv, sinv,
+                 macc, mrecv1, mrecv2, mrecv3, xsend, xrecv,
                  areca0, areca1, areca2, areca3, areca4, arecb0, arecb1, arecb2, arecb3, arecb4, gpart, gs0, gs1, gs2,
                  lsem, psem, s_qkv, s_mix, s_gm, s_dqkv, s_out, s_n2, s_gn2, s_feed, s_gb, s_blk, s_gn1, s_tok, g_sem,
                  mss, mrs, stsem, xs, ass, ars, bss, brs, gsem0, gsem1, gsem2):
@@ -457,7 +448,9 @@
 
     sum_o = GroupSum(me, low_a.at[0:256], (ra1, ra2), s_out, False)
     for j in range(2):
-        low_a[j * 128:(j + 1) * 128, :] = dot(mix[j * 128:(j + 1) * 128, :], wo[...]).astype(BF)
+        for n in range(4):
+            c = slice(n * 512, (n + 1) * 512)
+            low_a[j * 128:(j + 1) * 128, c] = dot(mix[j * 128:(j + 1) * 128, :], wo[:, c]).astype(BF)
         sum_o.send(j)
     p_out.wait()
     for i in range(3):
@@ -517,26 +510,26 @@
 
         mlp.append(Piece(me, lambda r, n=n: macc.at[n, r], dims, ("y0",),
                          (mrecv0.at[n], mrecv1.at[n], mrecv2.at[n], mrecv3.at[n]), mss.at[n], mrs.at[n], emit,
-                         stage.at[n % 2], stsem.at[n % 2]))
+                         [n2.at[:, pl.ds((n % 4) * 512 + a, 256)] for a in (0, 256)], stsem.at[n % 4]))
     four = range(4)
 
-    def outer(left, k, c):
-        t = left[:, c].T
+    def outer(left, k, n):
+        t = left[:, n * 512:(n + 1) * 512].T
         for weight in k:
             for i in range(3):
-                macc[slot[weight, i], c, :] = dot(t, hidden[weight * 3 + i]).astype(BF)
+                mlp[slot[weight, i]].put(n, dot(t, hidden[weight * 3 + i]).astype(BF))
 
     for n in four:
-        outer(g2, (0,), slice(n * 512, (n + 1) * 512))
+        outer(g2, (0,), n)
         if n % 2:
             sum2.step(n // 2, 0)
     for piece in (mlp[0], mlp[1], mlp[4]):
         piece.send(0)
     for n in four:
-        outer(n2, (1, 2), slice(n * 512, (n + 1) * 512))
+        outer(n2, (1, 2), n)
         if n % 2:
             sum2.step(n // 2, 1)
-    for piece in mlp[2:4] + mlp[5:8]:
+    for piece in mlp[2:4] + mlp[5:9]:
         piece.send(0)
     p_in = pltpu.make_async_copy(p_h, hidden.at[pl.ds(0, 8)], psem.at[1])
     for n in four:
@@ -573,6 +566,8 @@
     for j in range(2):
         gather_b.wait(j)
 
+    swap_mix.finish()
+    gm_s = mix_s
     for b in range(2):
         gmix = dot_nt(gb[...], wo[b * 256:(b + 1) * 256, :]).astype(BF)
         for s in range(2):
@@ -582,8 +577,7 @@
     swap_gm.start()
     for j in range(2):
         sumf.send(j)
-    mlp[8].send(0)
-
+    gather_n.finish()
     att_a, att_b = [], []
     spots = [(lambda r, i=i: wut.at[1 + i // 2, r, pl.ds((i % 2) * 128, 128)]) for i in range(4)]
     spots += [(lambda r, i=i: (wgt.at[i, r] if i < 3 else wut.at[0, r])) for i in range(4)]
@@ -601,8 +595,8 @@
     for j in four:
         c = slice(j * 512, (j + 1) * 512)
         v = dot(gb[:, c].T, mix[...]).astype(BF)
-        wut[1, c, :] = v[:, 0:256]
-        wut[2, c, :] = v[:, 256:512]
+        for i in range(4):
+            att_a[i].put(j, v[:, i * 128:(i + 1) * 128])
     for j in range(2):
         sumf.step(j, 0)
     for piece in att_a:
@@ -632,11 +626,8 @@
     swap_dqkv.start()
     for j in range(2):
         sumf.step(j, 1)
-    advance(mlp[0:4], 0)
-    gather_o = Gather(me, block_ref, s_blk, False)
-    for j in range(2):
-        block_ref[own_rows(me, j, False), :] = (mid_ref[halves(j), :] + sumf.step(j, 2)).astype(BF)
-        gather_o.start(j)
+    advance(mlp[0:2], 0)
+    advance(mlp[2:4], 0)
     advance(mlp[4:6], 0)
 
     def through_norm(grad_rot, pre, gain):
@@ -671,25 +662,27 @@
         gqkv[:, 768 + h * 128:896 + h * 128] = arrived(256, (2 * h, 2 * h + 1)).astype(BF)
     put_gain(33, gain_sum)
 
-    sum2.finish()
-    sum1 = GroupSum(me, low_a.at[0:256], (ra1, ra2), s_gn1, False)
-    for j in range(2):
-        r = slice(j * 128, (j + 1) * 128)
-        v = dot_nt(gqkv[r, 0:512], wq[...]) + dot_nt(gqkv[r, 512:768], wk[...]) + dot_nt(gqkv[r, 768:1024], wv[...])
-        low_a[r, :] = v.astype(BF)
-        sum1.send(j)
     for n in four:
         c = slice(n * 512, (n + 1) * 512)
         v = dot(n1[:, c].T, gqkv[...]).astype(BF)
-        for i in range(3):
-            wgt[i, c, :] = v[:, i * 256:(i + 1) * 256]
-        wut[0, c, :] = v[:, 768:1024]
+        for i in range(4):
+            att_b[i].put(n, v[:, i * 256:(i + 1) * 256])
     for piece in att_b:
         piece.send(0)
+    sum2.finish()
+    sum1 = GroupSum(me, low_a.at[0:256], (ra1, ra2), s_gn1, False)
+    for j in range(2):
+        r = slice(j * 128, (j + 1) * 128)
+        for n in four:
+            c = slice(n * 512, (n + 1) * 512)
+            v = dot_nt(gqkv[r, 0:512], wq[c, :]) + dot_nt(gqkv[r, 512:768], wk[c, :]) + dot_nt(gqkv[r, 768:1024], wv[c, :])
+            low_a[r, c] = v.astype(BF)
+        sum1.send(j)
+    advance(mlp[6:7], 0)
     for j in range(2):
         sum1.step(j, 0)
-    for j in range(2):
-        gather_o.relay(j)
+    advance(mlp[0:2] + mlp[4:5], 1)
+    advance(mlp[7:8], 0)
     scale1 = row_of(gain1)
     gather_t = Gather(me, tok_ref, s_tok, False)
     gain_term = jnp.zeros((1, 2048), F32)
@@ -706,31 +699,48 @@
     put_gain(0, gain_term)
     gains = GainSum(me, (gs0, gs1, gs2), (gsem0, gsem1, gsem2))
     gains.start(0, gpart[...])
-    advance(mlp[6:8], 0)
+    swap = [remote(xsend.at[n], xrecv.at[n], xs.at[n, 0], xs.at[n, 1], partner(me, "y0")) for n in range(9)]
+
+    def complete(first, last):
+        advance(mlp[first:last], 3)
+        for cp in swap[first:last]:
+            cp.start()
+
+    advance(mlp[2:4] + mlp[5:6], 1)
+    advance(att_a, 0)
+    gains.start(1, gains.take(0))
+    for j in range(2):
+        gather_t.relay(j)
+    advance(mlp[0:2], 2)
+    advance(mlp[6:8], 1)
     advance(mlp[8:9], 0)
-    advance(mlp[0:4], 1)
-    gains.start(1, gains.take(0))
-    for j in range(2):
-        gather_t.relay(j)
-    advance(att_a, 0)
-    advance(mlp[4:8], 1)
-    advance(att_b, 0)
+    advance(att_b[0:1], 0)
+    advance(att_b[2:4], 0)
+    advance(att_a, 1)
     gains.start(2, gains.take(1))
+    advance(mlp[2:6], 2)
+    gather_o = Gather(me, block_ref, s_blk, False)
+    for j in range(2):
+        block_ref[own_rows(me, j, False), :] = (mid_ref[halves(j), :] + sumf.step(j, 2)).astype(BF)
+        gather_o.start(j)
+    complete(0, 2)
+    advance(att_b[1:2], 0)
     advance(mlp[8:9], 1)
-    advance(att_a, 1)
-    advance(mlp, 2)
-    advance(att_b, 1)
-    advance(mlp, 3)
-    swap = [remote(xsend.at[n], xrecv.at[n], xs.at[n, 0], xs.at[n, 1], partner(me, "y0")) for n in range(9)]
-    for cp in swap:
-        cp.start()
+    advance(att_b[0:1] + att_b[2:4], 1)
+    advance(mlp[6:8], 2)
     advance(att_a, 2)
-    gains_ref[...] = gains.take(2)
+    complete(2, 6)
+    for j in range(2):
+        gather_o.relay(j)
+    advance(att_b[1:2], 1)
+    advance(mlp[8:9], 2)
     advance(att_b, 2)
+    complete(6, 9)
     advance(att_a, 3)
     advance(att_b, 3)
     advance(att_a, 4)
     advance(att_b, 4)
+    gains_ref[...] = gains.take(2)
     for n, cp in enumerate(swap):
         cp.wait_recv()
         k, i, _ = MLP_PIECES[n]
@@ -743,12 +753,10 @@
     for gather in (gather_o, gather_t):
         for j in range(2):
             gather.wait(j)
-    gather_n.finish()
     gains.finish()
     sum1.finish()
     for cp in g_copies:
         cp.wait_send()
-    swap_mix.finish()
     swap_gm.finish()
     swap_dqkv.finish()
     sumf.finish()
@@ -767,9 +775,9 @@
         layer_kernel,
         out_shape=(S((256, 2048), BF), S((256, 2048), BF), S((40, 128), F32),
                    S((2, 64, 768), F32), S((2, 64, 768), F32), S((2, 64, 768), F32), S((64, 512), F32), S((64, 512), F32),
-                   S((64, 256), F32), S((64, 256), F32), S((8, 512, 256), BF), S((9, 1024, 256), BF), S((9, 512, 256), BF)),
+                   S((64, 256), F32), S((64, 256), F32), S((8, 512, 256), BF), S((9, 1024, 256), BF)),
         in_specs=[A, A, V, V, V, V] + [A] * 9,
-        out_specs=(V,) * 10 + (A, A, A),
+        out_specs=(V,) * 10 + (A, A),
         scratch_shapes=[
             M((256, 2048), BF), M((256, 2048), BF), M((512, 2048), BF), M((512, 2048), BF),
             M((2048, 512), BF), M((2048, 256), BF), M((2048, 256), BF), M((512, 2048), BF),
@@ -777,19 +785,19 @@
             M((512, 2048), BF), M((512, 2048), BF),
             M((2, 4, 32, 2048), BF), M((2, 2, 32, 2048), BF), M((2, 1, 32, 2048), BF),
             M((2, 4, 32, 2048), BF), M((2, 2, 32, 2048), BF), M((2, 1, 32, 2048), BF), M((9, 512, 256), BF),
-            M((8, 128, 384), BF), M((8, 128, 384), BF), M((8, 128, 128), BF), M((8, 128, 128), BF), M((8, 128, 128), BF),
+            M((8, 128, 384), BF), M((8, 128, 384), BF), M((8, 128, 128), BF), M((8, 128, 128), BF),
             M((8, 128, 128), BF), M((8, 128, 384), BF), M((1024, 256), F32), M((256, 512), BF), M((256, 768), F32),
             M((256, 1024), BF), M((64, 2048), F32), M((64, 2048), F32),
             M((64, 2048), BF), M((128, 128), F32), M((128, 128), F32),
-            M((9, 2048, 256), BF), M((9, 256, 256), BF), M((9, 128, 256), BF),
-            M((2, 1024, 256), BF), M((9, 64, 256), BF), M((9, 64, 256), BF)]
+            M((9, 2048, 256), BF), M((9, 512, 256), BF), M((9, 256, 256), BF), M((9, 128, 256), BF),
+            M((9, 64, 256), BF), M((9, 64, 256), BF)]
         + [M((4, 1024 >> s, 128), BF) for s in range(5)] + [M((4, 1024 >> s, 256), BF) for s in range(5)]
         + [M((40, 128), F32), M((4, 40, 128), F32), M((8, 40, 128), F32), M((4, 40, 128), F32),
            D((16,)), D((2,)), D((2, 8)), D((2, 8)), D((2, 8)), D((2, 8)), D((2, 2, 2, 2)), D((2, 9, 2)), D((3, 2, 4, 2)),
            D((3, 2, 4, 2)), D((2, 3, 2)), D((2, 3, 2)), D((2, 2, 2, 2)), D((2, 3, 2)), D((2, 2)),
-           D((9, 4)), D((9, 4)), D((2,)), D((9, 2)), D((4, 5)), D((4, 5)), D((4, 5)), D((4, 5)),
+           D((9, 4)), D((9, 4)), D((4, 2)), D((9, 2)), D((4, 5)), D((4, 5)), D((4, 5)), D((4, 5)),
            D((2, 4)), D((2, 8)), D((2, 4))],
-        compiler_params=pltpu.CompilerParams(collective_id=3, has_side_effects=True, vmem_limit_bytes=63 * 2**20),
+        compiler_params=pltpu.CompilerParams(collective_id=3, has_side_effects=True, vmem_limit_bytes=127 * 2**19),
     )(x, g, gain1, gain2, qg, kg, wq, wk, wv, wo, wg, wu, wd, jnp.asarray(cos_t), jnp.asarray(sin_t))
 
 

time: 200 us -> 192 us (0.960)
  Pallas kernels: 199 us -> 191 us
    pallas_call x1, Pallas kernels: 194 us -> 186 us  [layer(): pl.pallas_call(layer_kernel, out_shape=(S((256, 2048), BF), S((256, 2048)...]
where the time goes in v1:
time: 192 us
  Pallas kernels  191 us (99%)
    pallas_call x1, Pallas kernels, layer(): pl.pallas_call(layer_kernel, out_shape=(S((256, 2048), BF), S((256, 2048)...  186 us
    pallas_call x1, Pallas kernels, tail(): pl.pallas_call(tail_kernel, out_shape=(S((256, 2048), BF), S((256, 2048),...  4.66 us

profile of v1, /device:TPU:0, one launch (start us, length us, event | category | flops | bytes accessed | tf_op | source)
XLA Modules:
  0.0 192.0 jit_solution(17770041247262177404)
XLA Ops:
  0.6 186.5 %shard_map.246 = (bf16[256,2048]{1,0:T(8,128)(2,1)}, bf16[256,2048]{1,0:T(8,128)(2,1)}, f32[40,128]{1,0:T(8,128)}, f32[2,64,768]{2,1,0:T(8,128)}, f32[2,64,768]{...) custom-call(bf16[256,2048]{1,0:T(8,128)(2,1)} %bitcast.10, ...), custom_call_target="tpu_custom_call" | custom-call | tf_op jit(solution)/shard_map/pallas_call | solution.py:774
  187.1 4.7 %shard_map.247 = (bf16[256,2048]{1,0:T(8,128)(2,1)}, bf16[256,2048]{1,0:T(8,128)(2,1)}, f32[16,128]{1,0:T(8,128)}, f32[64,512]{1,0:T(8,128)}, f32[64,256]{1,0:T(...) custom-call(bf16[256,2048]{1,0:T(8,128)(2,1)} %get-tuple-element.36., ...), custom_call_target="tpu_custom_call" | custom-call | tf_op jit(solution)/shard_map/pallas_call | solution.py:825

commit v2 on v1

--- a/solution.py
+++ b/solution.py
@@ -708,11 +708,11 @@
 
     advance(mlp[2:4] + mlp[5:6], 1)
     advance(att_a, 0)
-    gains.start(1, gains.take(0))
-    for j in range(2):
-        gather_t.relay(j)
     advance(mlp[0:2], 2)
     advance(mlp[6:8], 1)
+    gains.start(1, gains.take(0))
+    for j in range(2):
+        gather_t.relay(j)
     advance(mlp[8:9], 0)
     advance(att_b[0:1], 0)
     advance(att_b[2:4], 0)

time: 192 us -> 192 us (level)
  no operation moved by 1% of the time
where the time goes in v2:
time: 192 us
  Pallas kernels  191 us (99%)
    pallas_call x1, Pallas kernels, layer(): pl.pallas_call(layer_kernel, out_shape=(S((256, 2048), BF), S((256, 2048)...  186 us
    pallas_call x1, Pallas kernels, tail(): pl.pallas_call(tail_kernel, out_shape=(S((256, 2048), BF), S((256, 2048),...  4.66 us

profile of v2, /device:TPU:0, one launch (start us, length us, event | category | flops | bytes accessed | tf_op | source)
XLA Modules:
  0.0 191.7 jit_solution(4042087601859134487)
XLA Ops:
  0.6 186.2 %shard_map.246 = (bf16[256,2048]{1,0:T(8,128)(2,1)}, bf16[256,2048]{1,0:T(8,128)(2,1)}, f32[40,128]{1,0:T(8,128)}, f32[2,64,768]{2,1,0:T(8,128)}, f32[2,64,768]{...) custom-call(bf16[256,2048]{1,0:T(8,128)(2,1)} %bitcast.10, ...), custom_call_target="tpu_custom_call" | custom-call | tf_op jit(solution)/shard_map/pallas_call | solution.py:774
  186.8 4.7 %shard_map.247 = (bf16[256,2048]{1,0:T(8,128)(2,1)}, bf16[256,2048]{1,0:T(8,128)(2,1)}, f32[16,128]{1,0:T(8,128)}, f32[64,512]{1,0:T(8,128)}, f32[64,256]{1,0:T(...) custom-call(bf16[256,2048]{1,0:T(8,128)(2,1)} %get-tuple-element.36., ...), custom_call_target="tpu_custom_call" | custom-call | tf_op jit(solution)/shard_map/pallas_call | solution.py:825
